TPU v7x, 256 devices: a whole 4x4x8 slice. The times are simulated.
256 devices in a mesh: gen: 32 (over y, x, core), beam: 8 (over z).
Axes of the slice: x: 4, y: 4, z: 8, core: 2. Of those that a mesh axis runs over, the one named last changes fastest.
Arguments:
- gen_showers: bfloat16 [32768, 256], P('gen'), may hold values from -12 to 12
- beam_showers: bfloat16 [16384, 256], P('beam'), may hold values from -6 to 6
- embed_weight: bfloat16 [256, 128], replicated, may hold values from -0.375 to 0.375
- eps_roster: float32 [4], replicated, may hold values from 0.04 to 0.08
Outputs:
- gen_potential: float32 [32768], P('gen')
- beam_potential: float32 [16384], P('beam')
- weight_grad: float32 [256, 128], replicated
All inputs are finite; a program needn't handle non-finite values.
Results may differ from a plain program's by a relative error of at most 0.03.
Values sent between devices are 32-bit elements; how exact they have to be, the bound alone decides.
No kernel may reach another device: no remote copies, remote signals or barrier semaphores. Data moves between devices by JAX's collectives and lax.ppermute only.
A program may use at most 64 MiB of HBM per device.

v0:
```python
import math
import jax
import jax.numpy as jnp
from jax import lax
from jax.sharding import PartitionSpec as P

SWEEPS = 4


def embed(showers, weight):
    act = jnp.tanh(jnp.dot(showers, weight, preferred_element_type=jnp.float32))
    return (act, act.astype(jnp.bfloat16))


def tile_cost(gen_emb, beam_emb, gen_sq, beam_sq):
    cross = lax.dot_general(
        gen_emb, beam_emb, (((1,), (1,)), ((), ())), preferred_element_type=jnp.float32
    )
    return gen_sq[:, None] + beam_sq[None, :] - 2.0 * cross


def row_lse(scores):
    top = lax.pmax(jnp.max(scores, axis=1), "beam")
    total = lax.psum(jnp.sum(jnp.exp(scores - top[:, None]), axis=1), "beam")
    return top + jnp.log(total)


def col_lse(scores):
    top = lax.pmax(jnp.max(scores, axis=0), "gen")
    total = lax.psum(jnp.sum(jnp.exp(scores - top[None, :]), axis=0), "gen")
    return top + jnp.log(total)


def transpose_dot(left, right):
    return lax.dot_general(
        left.astype(jnp.float32),
        right,
        (((0,), (0,)), ((), ())),
        precision=lax.Precision.HIGHEST,
        preferred_element_type=jnp.float32,
    )


def on_device(gen_showers, beam_showers, embed_weight, eps_roster):
    gen_act, gen_emb = embed(gen_showers, embed_weight)
    beam_act, beam_emb = embed(beam_showers, embed_weight)
    gen_float = gen_emb.astype(jnp.float32)
    beam_float = beam_emb.astype(jnp.float32)
    gen_sq = jnp.sum(gen_float * gen_float, axis=1)
    beam_sq = jnp.sum(beam_float * beam_float, axis=1)
    rows = gen_emb.shape[0]
    columns = beam_emb.shape[0]
    log_beam = math.log(columns * lax.axis_size("beam"))
    log_gen = math.log(rows * lax.axis_size("gen"))
    beam_pot = jnp.zeros((columns,), jnp.float32)
    gen_pot = jnp.zeros((rows,), jnp.float32)
    for sweep in range(SWEEPS):
        temper = eps_roster[sweep]
        cost = tile_cost(gen_emb, beam_emb, gen_sq, beam_sq)
        gen_pot = temper * (log_beam - row_lse((beam_pot[None, :] - cost) / temper))
        cost = tile_cost(gen_emb, beam_emb, gen_sq, beam_sq)
        beam_pot = temper * (log_gen - col_lse((gen_pot[:, None] - cost) / temper))
    last = eps_roster[SWEEPS - 1]
    cost = tile_cost(gen_emb, beam_emb, gen_sq, beam_sq)
    mass = jnp.exp((gen_pot[:, None] + beam_pot[None, :] - cost) / last - log_beam)
    plan = mass.astype(jnp.bfloat16)
    gen_count = rows // lax.axis_size("beam")
    part = plan
    row_mass = jnp.sum(mass, axis=1)
    own = gen_float
    moved = jnp.dot(part, beam_emb, preferred_element_type=jnp.float32)
    grad_gen = lax.psum_scatter(
        2.0 * (row_mass[:, None] * own - moved), "beam", scatter_dimension=0, tiled=True
    )
    gen_start = lax.axis_index("beam") * gen_count
    act_rows = lax.dynamic_slice_in_dim(gen_act, gen_start, gen_count, 0)
    shower_rows = lax.dynamic_slice_in_dim(gen_showers, gen_start, gen_count, 0)
    beam_count = columns // lax.axis_size("gen")
    part = plan
    col_mass = jnp.sum(mass, axis=0)
    own = beam_float
    moved = lax.dot_general(
        part, gen_emb, (((0,), (0,)), ((), ())), preferred_element_type=jnp.float32
    )
    grad_beam = lax.psum_scatter(
        2.0 * (col_mass[:, None] * own - moved), "gen", scatter_dimension=0, tiled=True
    )
    beam_start = lax.axis_index("gen") * beam_count
    act_cols = lax.dynamic_slice_in_dim(beam_act, beam_start, beam_count, 0)
    shower_cols = lax.dynamic_slice_in_dim(beam_showers, beam_start, beam_count, 0)
    partial_grad = transpose_dot(shower_rows, grad_gen * (1.0 - act_rows * act_rows))
    partial_grad = partial_grad + transpose_dot(
        shower_cols, grad_beam * (1.0 - act_cols * act_cols)
    )
    weight_grad = lax.psum(partial_grad, ("gen", "beam"))
    return (gen_pot, beam_pot, weight_grad)


def solution(mesh):
    in_specs = (P("gen", None), P("beam", None), P(), P())
    out_specs = (P("gen"), P("beam"), P())
    return jax.shard_map(
        on_device, mesh=mesh, in_specs=in_specs, out_specs=out_specs, check_vma=False
    )
```

profile of v0, /device:TPU:8, one launch (start us, length us, event | category | flops | bytes accessed | tf_op | source)
XLA Modules:
  0.0 1114.6 jit_solution(14821040143072383777)
XLA Ops:
  7.2 0.0 copy-start
  7.2 0.0 reduce-scatter.5.cloned.1.call-start
  7.2 1.4 fusion.38
  8.6 1.4 fusion.14
  10.0 1.4 fusion.19
  11.4 5.3 fusion
  16.7 20.0 %pmax.56 = f32[1024]{0:T(1024)S(1)} all-reduce(f32[1024]{0:T(1024)S(1)} %get-tuple-element.16), channel_id=1, replica_groups=mesh['gen'=32,'beam'=8] {'beam'}, use_global_device_ids=true, to_apply=%region_3.0 | all-reduce | flops 1024 | bytes 8192 | tf_op jit(solution)/shard_map/pmax | solution.py:23
  36.7 5.1 exponential_reduce_fusion.7
  41.8 14.2 %psum.63 = f32[1024]{0:T(1024)S(1)} all-reduce(f32[1024]{0:T(1024)S(1)} %exponential_reduce_fusion.7), channel_id=1, replica_groups=mesh['gen'=32,'beam'=8] {'beam'}, use_global_device_ids=true, to_apply=%region_5.0 | all-reduce | flops 1024 | bytes 8192 | tf_op jit(solution)/shard_map/psum | solution.py:24
  56.0 0.7 subtract_multiply_fusion.7
  56.6 4.7 fusion.15
  61.3 54.0 %pmax.57 = f32[2048]{0:T(1024)S(1)} all-reduce(f32[2048]{0:T(1024)S(1)} %fusion.15), channel_id=1, replica_groups=mesh['gen'=32,'beam'=8] {'gen'}, use_global_device_ids=true, to_apply=%region_7.0 | all-reduce | flops 2048 | bytes 16384 | tf_op jit(solution)/shard_map/pmax | solution.py:29
  115.4 5.2 exponential_reduce_fusion.6
  120.5 55.5 %psum.64 = f32[2048]{0:T(1024)S(1)} all-reduce(f32[2048]{0:T(1024)S(1)} %exponential_reduce_fusion.6), channel_id=1, replica_groups=mesh['gen'=32,'beam'=8] {'gen'}, use_global_device_ids=true, to_apply=%region_9.0 | all-reduce | flops 2048 | bytes 16384 | tf_op jit(solution)/shard_map/psum | solution.py:30
  176.0 0.7 subtract_multiply_fusion.3
  176.7 4.8 fusion.1
  181.5 16.2 %pmax.58 = f32[1024]{0:T(1024)S(1)} all-reduce(f32[1024]{0:T(1024)S(1)} %fusion.1), channel_id=1, replica_groups=mesh['gen'=32,'beam'=8] {'beam'}, use_global_device_ids=true, to_apply=%region_11.0 | all-reduce | flops 1024 | bytes 8192 | tf_op jit(solution)/shard_map/pmax | solution.py:23
  197.7 5.1 exponential_reduce_fusion.5
  202.8 14.2 %psum.65 = f32[1024]{0:T(1024)S(1)} all-reduce(f32[1024]{0:T(1024)S(1)} %exponential_reduce_fusion.5), channel_id=1, replica_groups=mesh['gen'=32,'beam'=8] {'beam'}, use_global_device_ids=true, to_apply=%region_13.0 | all-reduce | flops 1024 | bytes 8192 | tf_op jit(solution)/shard_map/psum | solution.py:24
  217.0 0.6 subtract_multiply_fusion.6
  217.5 4.6 fusion.16
  222.1 63.7 %pmax.59 = f32[2048]{0:T(1024)S(1)} all-reduce(f32[2048]{0:T(1024)S(1)} %fusion.16), channel_id=1, replica_groups=mesh['gen'=32,'beam'=8] {'gen'}, use_global_device_ids=true, to_apply=%region_15.0 | all-reduce | flops 2048 | bytes 16384 | tf_op jit(solution)/shard_map/pmax | solution.py:29
  285.8 5.1 exponential_reduce_fusion.4
  290.9 63.7 %psum.66 = f32[2048]{0:T(1024)S(1)} all-reduce(f32[2048]{0:T(1024)S(1)} %exponential_reduce_fusion.4), channel_id=1, replica_groups=mesh['gen'=32,'beam'=8] {'gen'}, use_global_device_ids=true, to_apply=%region_17.0 | all-reduce | flops 2048 | bytes 16384 | tf_op jit(solution)/shard_map/psum | solution.py:30
  354.6 0.6 subtract_multiply_fusion.2
  355.2 4.9 fusion.2
  360.1 16.2 %pmax.60 = f32[1024]{0:T(1024)S(1)} all-reduce(f32[1024]{0:T(1024)S(1)} %fusion.2), channel_id=1, replica_groups=mesh['gen'=32,'beam'=8] {'beam'}, use_global_device_ids=true, to_apply=%region_19.0 | all-reduce | flops 1024 | bytes 8192 | tf_op jit(solution)/shard_map/pmax | solution.py:23
  376.3 5.1 exponential_reduce_fusion.3
  381.4 14.3 %psum.67 = f32[1024]{0:T(1024)S(1)} all-reduce(f32[1024]{0:T(1024)S(1)} %exponential_reduce_fusion.3), channel_id=1, replica_groups=mesh['gen'=32,'beam'=8] {'beam'}, use_global_device_ids=true, to_apply=%region_21.0 | all-reduce | flops 1024 | bytes 8192 | tf_op jit(solution)/shard_map/psum | solution.py:24
  395.8 0.7 subtract_multiply_fusion.5
  396.4 4.7 fusion.17
  401.1 63.7 %pmax.61 = f32[2048]{0:T(1024)S(1)} all-reduce(f32[2048]{0:T(1024)S(1)} %fusion.17), channel_id=1, replica_groups=mesh['gen'=32,'beam'=8] {'gen'}, use_global_device_ids=true, to_apply=%region_23.0 | all-reduce | flops 2048 | bytes 16384 | tf_op jit(solution)/shard_map/pmax | solution.py:29
  464.8 5.2 exponential_reduce_fusion.2
  470.0 63.7 %psum.68 = f32[2048]{0:T(1024)S(1)} all-reduce(f32[2048]{0:T(1024)S(1)} %exponential_reduce_fusion.2), channel_id=1, replica_groups=mesh['gen'=32,'beam'=8] {'gen'}, use_global_device_ids=true, to_apply=%region_25.0 | all-reduce | flops 2048 | bytes 16384 | tf_op jit(solution)/shard_map/psum | solution.py:30
  533.6 0.7 subtract_multiply_fusion.1
  534.3 4.9 fusion.3
  539.2 16.2 %pmax.62 = f32[1024]{0:T(1024)S(1)} all-reduce(f32[1024]{0:T(1024)S(1)} %fusion.3), channel_id=1, replica_groups=mesh['gen'=32,'beam'=8] {'beam'}, use_global_device_ids=true, to_apply=%region_27.0 | all-reduce | flops 1024 | bytes 8192 | tf_op jit(solution)/shard_map/pmax | solution.py:23
  555.4 5.1 exponential_reduce_fusion.1
  560.5 14.2 %psum.69 = f32[1024]{0:T(1024)S(1)} all-reduce(f32[1024]{0:T(1024)S(1)} %exponential_reduce_fusion.1), channel_id=1, replica_groups=mesh['gen'=32,'beam'=8] {'beam'}, use_global_device_ids=true, to_apply=%region_29.0 | all-reduce | flops 1024 | bytes 8192 | tf_op jit(solution)/shard_map/psum | solution.py:24
  574.7 0.7 subtract_multiply_fusion.4
  575.4 0.0 copy-start.2
  575.4 4.7 fusion.18
  580.0 63.7 %pmax.63 = f32[2048]{0:T(1024)S(1)} all-reduce(f32[2048]{0:T(1024)S(1)} %fusion.18), channel_id=1, replica_groups=mesh['gen'=32,'beam'=8] {'gen'}, use_global_device_ids=true, to_apply=%region_31.0 | all-reduce | flops 2048 | bytes 16384 | tf_op jit(solution)/shard_map/pmax | solution.py:29
  643.7 5.2 exponential_reduce_fusion
  648.9 63.7 %psum.70 = f32[2048]{0:T(1024)S(1)} all-reduce(f32[2048]{0:T(1024)S(1)} %exponential_reduce_fusion), channel_id=1, replica_groups=mesh['gen'=32,'beam'=8] {'gen'}, use_global_device_ids=true, to_apply=%region_33.0 | all-reduce | flops 2048 | bytes 16384 | tf_op jit(solution)/shard_map/psum | solution.py:30
  712.6 0.7 subtract_multiply_fusion
  713.3 0.0 copy-done.2
  713.3 0.0 copy-start.3
  713.3 5.7 fusion.37
  719.0 0.0 copy-start.1
  719.0 1.9 copy-done.1
  720.9 2.4 fusion.4
  723.3 0.0 reduce-scatter.5.cloned.1.call-update
  723.3 0.0 reduce-scatter.3.cloned.1.call-start
  723.4 4.5 fusion.11
  727.9 0.0 reduce-scatter.3.cloned.1.call-update
  727.9 0.0 all-reduce.2.cloned.1.call-start
  728.0 92.3 %reduce-scatter.5.cloned.1.call-done = f32[64,128]{1,0:T(8,128)} async-done(((f32[2048,128]{1,0:T(8,128)}), f32[64,128]{1,0:T(8,128)}) %reduce-scatter.5.cloned.1.call-update) | async-done | bytes 32784 | tf_op jit(solution)/shard_map/reduce_scatter | solution.py:85
  820.2 1.0 fusion.25
  821.3 38.7 %reduce-scatter.3.cloned.1.call-done = f32[128,128]{0,1:T(8,128)} async-done(((f32[1024,128]{0,1:T(8,128)}), f32[128,128]{0,1:T(8,128)}) %reduce-scatter.3.cloned.1.call-update) | async-done | bytes 65552 | tf_op jit(solution)/shard_map/reduce_scatter | solution.py:72
  859.9 1.8 convolution_add_fusion
  861.7 0.0 all-reduce.2.cloned.1.call-update
  861.7 244.8 %all-reduce.2.cloned.1.call-done = f32[256,128]{1,0:T(8,128)} async-done(((f32[256,128]{1,0:T(8,128)}), f32[256,128]{1,0:T(8,128)}) %all-reduce.2.cloned.1.call-update) | async-done | bytes 131088 | tf_op jit(solution)/shard_map/psum | solution.py:95
  1106.5 1.6 copy.8
  (2 shorter events, 0.0 us)
Async XLA Ops:
  7.2 1.5 copy-start
  7.2 813.0 %reduce-scatter.5.cloned.1.call-start = ((), (), s32[]{:S(2)}) async-start(), calls=%async_computation.3 | async-start | bytes 1081344 | tf_op jit(solution)/shard_map/reduce_scatter | solution.py:85
  575.4 137.9 %copy-start.2 = (f32[1024]{0:T(1024)}, f32[1024]{0:T(1024)S(1)}, u32[]{:S(2)}) copy-start(f32[1024]{0:T(1024)S(1)} %subtract_multiply_fusion.4) | copy-start | bytes 12292
  713.3 10.0 copy-start.3
  719.0 1.9 copy-start.1
  723.3 136.6 %reduce-scatter.3.cloned.1.call-start = ((), (), s32[]{:S(2)}) async-start(), calls=%async_computation.2 | async-start | bytes 589824 | tf_op jit(solution)/shard_map/reduce_scatter | solution.py:72
  727.9 378.6 %all-reduce.2.cloned.1.call-start = ((), (), s32[]{:S(2)}) async-start(), calls=%async_computation.4 | async-start | bytes 262144 | tf_op jit(solution)/shard_map/psum | solution.py:95
Sparse Core Ops, SparseCore 0:
  723.5 96.7 reduce-scatter.4
  822.9 36.9 reduce-scatter.2
  866.0 240.4 all-reduce.1
where the time goes:
time: 1120 us; the launch traced here: 1110 us
  blocking collectives  617 us (55%)
  waiting for transfers between devices  376 us (34%)
  other arithmetic  85 us (8%)
  matrix products  17.8 us (2%)
  between operations  14 us (1%)
    psum x4, blocking collectives, col_lse(): total = lax.psum(jnp.sum(jnp.exp(scores - top[None, :]), axis=0), 'gen')  247 us
    pmax x4, blocking collectives, col_lse(): top = lax.pmax(jnp.max(scores, axis=0), 'gen')  245 us
    psum x1, waiting for transfers between devices, on_device(): weight_grad = lax.psum(partial_grad, ('gen', 'beam'))  245 us
    reduce_scatter x1, waiting for transfers between devices, on_device(): lax.psum_scatter(2.0 * (col_mass[:, None] * own - moved), 'gen', scatter_...  92.3 us
    pmax x4, blocking collectives, row_lse(): top = lax.pmax(jnp.max(scores, axis=1), 'beam')  68.5 us
    psum x4, blocking collectives, row_lse(): total = lax.psum(jnp.sum(jnp.exp(scores - top[:, None]), axis=1), 'beam')  56.8 us
    reduce_scatter x1, waiting for transfers between devices, on_device(): lax.psum_scatter(2.0 * (row_mass[:, None] * own - moved), 'beam', scatter...  38.7 us
  transfers between devices with their start and end apart: 3, of which 3 were waited for; matrix products, arithmetic and copies ran while one was open for 0% of the time, Pallas kernels for 0%

commit v1 on v0

--- a/solution.py
+++ b/solution.py
@@ -92,7 +92,9 @@
     partial_grad = partial_grad + transpose_dot(
         shower_cols, grad_beam * (1.0 - act_cols * act_cols)
     )
-    weight_grad = lax.psum(partial_grad, ("gen", "beam"))
+    weight_grad = partial_grad
+    for name in ("beam", "gen"):
+        weight_grad = lax.psum(weight_grad, name)
     return (gen_pot, beam_pot, weight_grad)
 
 

time: 1120 us -> 1060 us (0.946)
  waiting for transfers between devices: 376 us -> 314 us
    psum x1 -> x2, waiting for transfers between devices: 245 us -> 183 us  [on_device(): weight_grad = lax.psum(weight_grad, name)]
  transfers between devices with their start and end apart: 3 -> 4, of which waited for: 3 -> 4; matrix products, arithmetic and copies ran while one was open for 0% -> 1% of each run, Pallas kernels for 0% -> 0%
where the time goes in v1:
time: 1060 us; the launch traced here: 1050 us
  blocking collectives  617 us (58%)
  waiting for transfers between devices  314 us (30%)
  other arithmetic  85 us (8%)
  matrix products  17.8 us (2%)
  between operations  14 us (1%)
    psum x4, blocking collectives, col_lse(): total = lax.psum(jnp.sum(jnp.exp(scores - top[None, :]), axis=0), 'gen')  247 us
    pmax x4, blocking collectives, col_lse(): top = lax.pmax(jnp.max(scores, axis=0), 'gen')  245 us
    psum x2, waiting for transfers between devices, on_device(): weight_grad = lax.psum(weight_grad, name)  183 us
    reduce_scatter x1, waiting for transfers between devices, on_device(): lax.psum_scatter(2.0 * (col_mass[:, None] * own - moved), 'gen', scatter_...  92.3 us
    pmax x4, blocking collectives, row_lse(): top = lax.pmax(jnp.max(scores, axis=1), 'beam')  68.5 us
    psum x4, blocking collectives, row_lse(): total = lax.psum(jnp.sum(jnp.exp(scores - top[:, None]), axis=1), 'beam')  56.8 us
    reduce_scatter x1, waiting for transfers between devices, on_device(): lax.psum_scatter(2.0 * (row_mass[:, None] * own - moved), 'beam', scatter...  38.7 us
  transfers between devices with their start and end apart: 4, of which 4 were waited for; matrix products, arithmetic and copies ran while one was open for 1% of the time, Pallas kernels for 0%

profile of v1, /device:TPU:8, one launch (start us, length us, event | category | flops | bytes accessed | tf_op | source)
XLA Modules:
  0.0 1052.6 jit_solution(6541852075510185726)
XLA Ops:
  7.2 0.0 copy-start
  7.2 0.0 reduce-scatter.5.cloned.1.call-start
  7.2 1.4 fusion.38
  8.6 1.4 fusion.14
  10.0 1.4 fusion.19
  11.4 5.3 fusion
  16.7 20.0 %pmax.56 = f32[1024]{0:T(1024)S(1)} all-reduce(f32[1024]{0:T(1024)S(1)} %get-tuple-element.16), channel_id=1, replica_groups=mesh['gen'=32,'beam'=8] {'beam'}, use_global_device_ids=true, to_apply=%region_3.0 | all-reduce | flops 1024 | bytes 8192 | tf_op jit(solution)/shard_map/pmax | solution.py:23
  36.7 5.1 exponential_reduce_fusion.7
  41.8 14.2 %psum.70 = f32[1024]{0:T(1024)S(1)} all-reduce(f32[1024]{0:T(1024)S(1)} %exponential_reduce_fusion.7), channel_id=1, replica_groups=mesh['gen'=32,'beam'=8] {'beam'}, use_global_device_ids=true, to_apply=%region_5.0 | all-reduce | flops 1024 | bytes 8192 | tf_op jit(solution)/shard_map/psum | solution.py:24
  56.0 0.7 subtract_multiply_fusion.7
  56.6 4.7 fusion.15
  61.3 54.0 %pmax.57 = f32[2048]{0:T(1024)S(1)} all-reduce(f32[2048]{0:T(1024)S(1)} %fusion.15), channel_id=1, replica_groups=mesh['gen'=32,'beam'=8] {'gen'}, use_global_device_ids=true, to_apply=%region_7.0 | all-reduce | flops 2048 | bytes 16384 | tf_op jit(solution)/shard_map/pmax | solution.py:29
  115.4 5.2 exponential_reduce_fusion.6
  120.5 55.5 %psum.71 = f32[2048]{0:T(1024)S(1)} all-reduce(f32[2048]{0:T(1024)S(1)} %exponential_reduce_fusion.6), channel_id=1, replica_groups=mesh['gen'=32,'beam'=8] {'gen'}, use_global_device_ids=true, to_apply=%region_9.0 | all-reduce | flops 2048 | bytes 16384 | tf_op jit(solution)/shard_map/psum | solution.py:30
  176.0 0.7 subtract_multiply_fusion.3
  176.7 4.8 fusion.1
  181.5 16.2 %pmax.58 = f32[1024]{0:T(1024)S(1)} all-reduce(f32[1024]{0:T(1024)S(1)} %fusion.1), channel_id=1, replica_groups=mesh['gen'=32,'beam'=8] {'beam'}, use_global_device_ids=true, to_apply=%region_11.0 | all-reduce | flops 1024 | bytes 8192 | tf_op jit(solution)/shard_map/pmax | solution.py:23
  197.7 5.1 exponential_reduce_fusion.5
  202.8 14.2 %psum.72 = f32[1024]{0:T(1024)S(1)} all-reduce(f32[1024]{0:T(1024)S(1)} %exponential_reduce_fusion.5), channel_id=1, replica_groups=mesh['gen'=32,'beam'=8] {'beam'}, use_global_device_ids=true, to_apply=%region_13.0 | all-reduce | flops 1024 | bytes 8192 | tf_op jit(solution)/shard_map/psum | solution.py:24
  217.0 0.6 subtract_multiply_fusion.6
  217.5 4.6 fusion.16
  222.1 63.7 %pmax.59 = f32[2048]{0:T(1024)S(1)} all-reduce(f32[2048]{0:T(1024)S(1)} %fusion.16), channel_id=1, replica_groups=mesh['gen'=32,'beam'=8] {'gen'}, use_global_device_ids=true, to_apply=%region_15.0 | all-reduce | flops 2048 | bytes 16384 | tf_op jit(solution)/shard_map/pmax | solution.py:29
  285.8 5.1 exponential_reduce_fusion.4
  290.9 63.7 %psum.73 = f32[2048]{0:T(1024)S(1)} all-reduce(f32[2048]{0:T(1024)S(1)} %exponential_reduce_fusion.4), channel_id=1, replica_groups=mesh['gen'=32,'beam'=8] {'gen'}, use_global_device_ids=true, to_apply=%region_17.0 | all-reduce | flops 2048 | bytes 16384 | tf_op jit(solution)/shard_map/psum | solution.py:30
  354.6 0.6 subtract_multiply_fusion.2
  355.2 4.9 fusion.2
  360.1 16.2 %pmax.60 = f32[1024]{0:T(1024)S(1)} all-reduce(f32[1024]{0:T(1024)S(1)} %fusion.2), channel_id=1, replica_groups=mesh['gen'=32,'beam'=8] {'beam'}, use_global_device_ids=true, to_apply=%region_19.0 | all-reduce | flops 1024 | bytes 8192 | tf_op jit(solution)/shard_map/pmax | solution.py:23
  376.3 5.1 exponential_reduce_fusion.3
  381.4 14.3 %psum.74 = f32[1024]{0:T(1024)S(1)} all-reduce(f32[1024]{0:T(1024)S(1)} %exponential_reduce_fusion.3), channel_id=1, replica_groups=mesh['gen'=32,'beam'=8] {'beam'}, use_global_device_ids=true, to_apply=%region_21.0 | all-reduce | flops 1024 | bytes 8192 | tf_op jit(solution)/shard_map/psum | solution.py:24
  395.8 0.7 subtract_multiply_fusion.5
  396.4 4.7 fusion.17
  401.1 63.7 %pmax.61 = f32[2048]{0:T(1024)S(1)} all-reduce(f32[2048]{0:T(1024)S(1)} %fusion.17), channel_id=1, replica_groups=mesh['gen'=32,'beam'=8] {'gen'}, use_global_device_ids=true, to_apply=%region_23.0 | all-reduce | flops 2048 | bytes 16384 | tf_op jit(solution)/shard_map/pmax | solution.py:29
  464.8 5.2 exponential_reduce_fusion.2
  470.0 63.7 %psum.75 = f32[2048]{0:T(1024)S(1)} all-reduce(f32[2048]{0:T(1024)S(1)} %exponential_reduce_fusion.2), channel_id=1, replica_groups=mesh['gen'=32,'beam'=8] {'gen'}, use_global_device_ids=true, to_apply=%region_25.0 | all-reduce | flops 2048 | bytes 16384 | tf_op jit(solution)/shard_map/psum | solution.py:30
  533.6 0.7 subtract_multiply_fusion.1
  534.3 4.9 fusion.3
  539.2 16.2 %pmax.62 = f32[1024]{0:T(1024)S(1)} all-reduce(f32[1024]{0:T(1024)S(1)} %fusion.3), channel_id=1, replica_groups=mesh['gen'=32,'beam'=8] {'beam'}, use_global_device_ids=true, to_apply=%region_27.0 | all-reduce | flops 1024 | bytes 8192 | tf_op jit(solution)/shard_map/pmax | solution.py:23
  555.4 5.1 exponential_reduce_fusion.1
  560.5 14.2 %psum.76 = f32[1024]{0:T(1024)S(1)} all-reduce(f32[1024]{0:T(1024)S(1)} %exponential_reduce_fusion.1), channel_id=1, replica_groups=mesh['gen'=32,'beam'=8] {'beam'}, use_global_device_ids=true, to_apply=%region_29.0 | all-reduce | flops 1024 | bytes 8192 | tf_op jit(solution)/shard_map/psum | solution.py:24
  574.7 0.7 subtract_multiply_fusion.4
  575.4 4.7 fusion.18
  580.0 63.7 %pmax.63 = f32[2048]{0:T(1024)S(1)} all-reduce(f32[2048]{0:T(1024)S(1)} %fusion.18), channel_id=1, replica_groups=mesh['gen'=32,'beam'=8] {'gen'}, use_global_device_ids=true, to_apply=%region_31.0 | all-reduce | flops 2048 | bytes 16384 | tf_op jit(solution)/shard_map/pmax | solution.py:29
  643.7 5.2 exponential_reduce_fusion
  648.9 63.7 %psum.77 = f32[2048]{0:T(1024)S(1)} all-reduce(f32[2048]{0:T(1024)S(1)} %exponential_reduce_fusion), channel_id=1, replica_groups=mesh['gen'=32,'beam'=8] {'gen'}, use_global_device_ids=true, to_apply=%region_33.0 | all-reduce | flops 2048 | bytes 16384 | tf_op jit(solution)/shard_map/psum | solution.py:30
  712.6 0.7 subtract_multiply_fusion
  713.3 0.0 copy-start.3
  713.3 5.7 fusion.37
  719.0 1.9 copy-done.1
  720.9 2.4 fusion.4
  723.3 0.0 reduce-scatter.5.cloned.1.call-update
  723.3 0.0 reduce-scatter.3.cloned.1.call-start
  723.4 4.5 fusion.11
  727.9 0.0 reduce-scatter.3.cloned.1.call-update
  727.9 0.0 all-reduce.3.cloned.1.call-start
  728.0 92.3 %reduce-scatter.5.cloned.1.call-done = f32[64,128]{1,0:T(8,128)} async-done(((f32[2048,128]{1,0:T(8,128)}), f32[64,128]{1,0:T(8,128)}) %reduce-scatter.5.cloned.1.call-update) | async-done | bytes 32784 | tf_op jit(solution)/shard_map/reduce_scatter | solution.py:85
  820.2 1.0 fusion.25
  821.3 38.7 %reduce-scatter.3.cloned.1.call-done = f32[128,128]{0,1:T(8,128)} async-done(((f32[1024,128]{0,1:T(8,128)}), f32[128,128]{0,1:T(8,128)}) %reduce-scatter.3.cloned.1.call-update) | async-done | bytes 65552 | tf_op jit(solution)/shard_map/reduce_scatter | solution.py:72
  859.9 1.8 convolution_add_fusion
  861.7 0.0 all-reduce.3.cloned.1.call-update
  861.7 0.0 all-reduce.5.cloned.1.call-start
  861.8 71.5 %all-reduce.3.cloned.1.call-done = f32[256,128]{1,0:T(8,128)} async-done(((f32[256,128]{1,0:T(8,128)}), f32[256,128]{1,0:T(8,128)}) %all-reduce.3.cloned.1.call-update) | async-done | bytes 131088 | tf_op jit(solution)/shard_map/psum | solution.py:97
  933.3 0.0 all-reduce.5.cloned.1.call-update
  933.4 111.1 %all-reduce.5.cloned.1.call-done = f32[256,128]{1,0:T(8,128)} async-done(((f32[256,128]{1,0:T(8,128)}), f32[256,128]{1,0:T(8,128)}) %all-reduce.5.cloned.1.call-update) | async-done | bytes 131088 | tf_op jit(solution)/shard_map/psum | solution.py:97
  1044.5 1.6 copy.9
  (5 shorter events, 0.0 us)
Async XLA Ops:
  7.2 1.5 copy-start
  7.2 813.0 %reduce-scatter.5.cloned.1.call-start = ((), (), s32[]{:S(2)}) async-start(), calls=%async_computation.3 | async-start | bytes 1081344 | tf_op jit(solution)/shard_map/reduce_scatter | solution.py:85
  575.4 137.9 %copy-start.2 = (f32[1024]{0:T(1024)}, f32[1024]{0:T(1024)S(1)}, u32[]{:S(2)}) copy-start(f32[1024]{0:T(1024)S(1)} %subtract_multiply_fusion.4) | copy-start | bytes 12292
  713.3 10.0 copy-start.3
  719.0 1.9 copy-start.1
  723.3 136.6 %reduce-scatter.3.cloned.1.call-start = ((), (), s32[]{:S(2)}) async-start(), calls=%async_computation.2 | async-start | bytes 589824 | tf_op jit(solution)/shard_map/reduce_scatter | solution.py:72
  727.9 205.4 %all-reduce.3.cloned.1.call-start = ((), (), s32[]{:S(2)}) async-start(), calls=%async_computation.4 | async-start | bytes 262144 | tf_op jit(solution)/shard_map/psum | solution.py:97
  861.7 182.8 %all-reduce.5.cloned.1.call-start = ((), (), s32[]{:S(2)}) async-start(), calls=%async_computation.5 | async-start | bytes 262144 | tf_op jit(solution)/shard_map/psum | solution.py:97
Sparse Core Ops, SparseCore 0:
  723.5 96.7 reduce-scatter.4
  822.9 36.9 reduce-scatter.2
  862.8 70.4 all-reduce.2
  936.7 107.7 all-reduce.4
